TPU v7x, 512 devices: a whole 4x4x16 slice. The times are simulated.
512 devices in a mesh: region: 128 (over y, z, core), lev: 4 (over x).
Axes of the slice: x: 4, y: 4, z: 16, core: 2. Of those that a mesh axis runs over, the one named last changes fastest.
Arguments:
- background_members: bfloat16 [80, 16, 1024, 128], P(None, 'lev', 'region'), may hold values from -6 to 6
- channel_height_kernel: float32 [8, 16], P(None, 'lev'), may hold values from -1.5 to 1.5
- sensor_spread_down: float32 [4], replicated, may hold values from 0.2 to 0.6
- sensor_spread_across: float32 [4], replicated, may hold values from 0.2 to 0.6
- measurement_placement: int32 [4, 64], replicated, may hold values from 0 to 511
- measurement_ordering: int32 [4, 64], replicated, may hold values from 0 to 63, each once within a row
- group_area_number: int32 [4], replicated, may hold values from 0 to 127
- taper_radius_limit: int32 [8], replicated, may hold values from 128 to 256
- measured_amounts: float32 [4, 64], replicated, may hold values from -8 to 8
- measurement_noise_spread: float32 [4, 64], replicated, may hold values from 0.05 to 0.5
Outputs:
- analysis: bfloat16 [80, 16, 128, 1024], P(None, 'lev', 'region')
All inputs are finite; a program needn't handle non-finite values.
Results may differ from a plain program's by a relative error of at most 0.001.
Values may be sent and summed in bfloat16 or wider, within the bound.
A program may use at most 128 MiB of HBM per device.

v0:
```python
import jax
import jax.numpy as jnp
from jax import lax
from jax.sharding import PartitionSpec as P

TILE = 32
STRIDE = 4


highest = lax.Precision.HIGHEST
group_width = 32


def copy_for_each(shard, axis):
    copies = jnp.broadcast_to(shard, (lax.axis_size(axis), *shard.shape))
    return lax.all_to_all(copies, axis, split_axis=0, concat_axis=0, tiled=True)


def over_copies(shard, axis):
    return copy_for_each(shard, axis).sum(axis=0)


def over_pieces(shard, axis):
    tiles = lax.all_gather(shard, axis)
    return tiles.sum(axis=0)


def footprint(present_state_grid, sensor_spread_down, sensor_spread_across, channel_height_kernel):
    members, levels, pixels = present_state_grid.shape
    foot_cells = TILE // STRIDE
    tiles_view = present_state_grid.reshape(members, levels, foot_cells, STRIDE, foot_cells, STRIDE)
    blocks = jnp.einsum(
        "klaicj,i,j->klac", tiles_view, sensor_spread_down, sensor_spread_across, precision=highest
    )
    blocks = blocks.reshape(members, levels, foot_cells * foot_cells)
    weighted = jnp.einsum("klq,hl->khq", blocks, channel_height_kernel, precision=highest)
    return weighted.reshape(members, -1)


def taper_weight(distance, cut_radius):
    return jnp.maximum(0.0, 1.0 - distance / (cut_radius + 1.0))


def serial_block(current, values, errors):
    denominator = current.shape[0] - 1.0
    recorded = []
    for column_id in range(current.shape[1]):
        column = current[:, column_id]
        center_col = jnp.mean(column)
        anomaly_col = column - center_col
        variance = jnp.sum(anomaly_col * anomaly_col) / denominator + errors[column_id]
        alpha_gain = 1.0 / (1.0 + jnp.sqrt(errors[column_id] / variance))
        innovation = values[column_id] - center_col
        recorded.append(column)
        anomaly_all = current - jnp.mean(current, axis=0, keepdims=True)
        covariance = jnp.dot(anomaly_col, anomaly_all, precision=highest) / denominator
        current = current + jnp.outer(innovation - alpha_gain * anomaly_col, covariance / variance)
    return jnp.stack(recorded, axis=1)


def block_terms(recorded, values, errors):
    denominator = recorded.shape[0] - 1.0
    center_blk = jnp.mean(recorded, axis=0)
    anomaly_rec = recorded - center_blk[None]
    variance = jnp.sum(anomaly_rec * anomaly_rec, axis=0) / denominator + errors
    alpha_gain = 1.0 / (1.0 + jnp.sqrt(errors / variance))
    scale_pert = alpha_gain / (denominator * variance)
    scale_mean = (values - center_blk) / (denominator * variance)
    return (anomaly_rec, scale_pert, scale_mean)


def advance(transforms, offsets, anomaly_rec, scale_pert, scale_mean, tapers):
    block_size = anomaly_rec.shape[1]
    gram_matrix = jnp.dot(anomaly_rec.T, anomaly_rec, precision=highest)
    upper_part = jnp.triu(gram_matrix, 1)
    coef_pert = tapers * scale_pert[None]
    coef_mean = tapers * scale_mean[None]
    identity_blk = jnp.eye(block_size, dtype=jnp.float32)[None]
    nilpotent = coef_pert[:, :, None] * upper_part[None]
    inverse = identity_blk - nilpotent
    power = nilpotent
    for level_id in range((block_size - 1).bit_length() - 1):
        power = jnp.einsum("tij,tjk->tik", power, power, precision=highest)
        inverse = inverse + jnp.einsum("tij,tjk->tik", inverse, power, precision=highest)
    factor = inverse * coef_pert[:, None, :]
    carried = jnp.einsum("ij,tj->ti", upper_part, coef_mean, precision=highest)
    weights_mean = coef_mean - jnp.einsum("tij,tj->ti", factor, carried, precision=highest)
    mapped = jnp.einsum("tkm,mj->tkj", transforms, anomaly_rec, precision=highest)
    offsets = offsets + jnp.einsum("tkj,tj->tk", mapped, weights_mean, precision=highest)
    folded = jnp.einsum("tkj,tjl->tkl", mapped, factor, precision=highest)
    transforms = transforms - jnp.einsum("tkl,ml->tkm", folded, anomaly_rec, precision=highest)
    return (transforms, offsets)


def run_batch(base_priors, values, errors, transforms, offsets, tapers, target):
    center = jnp.mean(base_priors, axis=0)
    anomaly = base_priors - center[None]
    count_blocks = base_priors.shape[1] // group_width

    def one_block(block_id, state_carry):
        transforms, offsets, recorded_all = state_carry
        start = block_id * group_width
        anomaly_blk = lax.dynamic_slice_in_dim(anomaly, start, group_width, 1)
        center_blk = lax.dynamic_slice_in_dim(center, start, group_width, 0)
        values_blk = lax.dynamic_slice_in_dim(values, start, group_width, 0)
        errors_blk = lax.dynamic_slice_in_dim(errors, start, group_width, 0)
        tapers_blk = lax.dynamic_slice_in_dim(tapers, start, group_width, 1)
        current = (
            jnp.dot(transforms[target].T, anomaly_blk, precision=highest)
            + (center_blk + jnp.dot(offsets[target], anomaly_blk, precision=highest))[None]
        )
        recorded = serial_block(current, values_blk, errors_blk)
        anomaly_rec, scale_pert, scale_mean = block_terms(recorded, values_blk, errors_blk)
        transforms, offsets = advance(
            transforms, offsets, anomaly_rec, scale_pert, scale_mean, tapers_blk
        )
        recorded_all = lax.dynamic_update_slice_in_dim(recorded_all, recorded, start, 1)
        return (transforms, offsets, recorded_all)

    return lax.fori_loop(
        0, count_blocks, one_block, (transforms, offsets, jnp.zeros_like(base_priors))
    )


def body(
    background_members,
    channel_height_kernel,
    sensor_spread_down,
    sensor_spread_across,
    measurement_placement,
    measurement_ordering,
    group_area_number,
    taper_radius_limit,
    measured_amounts,
    measurement_noise_spread,
):
    own_region = lax.axis_index("region")
    present_state_grid = lax.all_to_all(
        background_members, "region", split_axis=3, concat_axis=2, tiled=True
    )[:, :, :, 0].astype(jnp.float32)
    present_state_grid, partial_priors = (
        present_state_grid,
        footprint(
            present_state_grid, sensor_spread_down, sensor_spread_across, channel_height_kernel
        ),
    )
    priors = over_copies(partial_priors, "lev")
    members, levels, pixels = present_state_grid.shape
    flat_field = present_state_grid.reshape(members, levels * pixels)
    center = jnp.mean(flat_field, axis=0)
    anomaly = flat_field - center[None]
    picked = jnp.take_along_axis(measurement_placement, measurement_ordering, axis=1)
    values_all = jnp.take_along_axis(measured_amounts, measurement_ordering, axis=1)
    errors_all = jnp.take_along_axis(measurement_noise_spread, measurement_ordering, axis=1)
    foot_cells = TILE // STRIDE * (TILE // STRIDE)
    channels = picked // foot_cells
    channel_ids = jnp.arange(taper_radius_limit.shape[0], dtype=jnp.int32)
    cut_radius = jnp.sum(
        jnp.where(channels[:, :, None] == channel_ids, taper_radius_limit, 0), axis=2
    ).astype(jnp.float32)
    batches = measurement_placement.shape[0]
    eye_members = jnp.eye(members, dtype=jnp.float32)
    hosting = own_region == group_area_number
    chosen = jnp.take(priors, picked.reshape(-1), axis=1).reshape(members, batches, -1)
    chosen = jnp.where(hosting[None, :, None], chosen, 0.0)
    bases = over_pieces(chosen, "region")
    targets = jnp.concatenate([own_region[None], group_area_number])
    count_targets = batches + 1
    transforms = jnp.tile(eye_members[None], (count_targets, 1, 1))
    offsets = jnp.zeros((count_targets, members), jnp.float32)
    for batch_id in range(batches):
        distance = jnp.abs(targets - group_area_number[batch_id]).astype(jnp.float32)
        tapers = taper_weight(distance[:, None], cut_radius[batch_id][None])
        outcome = run_batch(
            bases[:, batch_id],
            values_all[batch_id],
            errors_all[batch_id],
            transforms,
            offsets,
            tapers,
            1 + batch_id,
        )
        transforms, offsets = (outcome[0], outcome[1])
    mixing = transforms[0] + offsets[0][:, None]
    result = jnp.dot(mixing.T, anomaly, precision=highest) + center[None]
    return result.reshape(members, levels, 1, pixels).astype(jnp.bfloat16)


def solution(mesh):
    return jax.shard_map(
        body,
        mesh=mesh,
        in_specs=(
            P(None, "lev", "region", None),
            P(None, "lev"),
            P(),
            P(),
            P(),
            P(),
            P(),
            P(),
            P(),
            P(),
        ),
        out_specs=P(None, "lev", "region", None),
        check_vma=False,
    )
```

profile of v0, /device:TPU:1, one launch (start us, length us, event | category | flops | bytes accessed | tf_op | source)
XLA Modules:
  0.0 1575.1 jit_solution(12784982032476468908)
XLA Ops:
  6.5 3.0 copy.33
  9.6 20.7 %all-to-all-start = ((bf16[80,4,8,128]{0,2,1,3:T(8,128)(2,1)}), bf16[80,4,8,128]{0,2,1,3:T(8,128)(2,1)S(1)}, u32[]{:S(2)}, u32[]{:S(2)}) async-start(bf16[80,4,8,128]{0,2,1,3:T(8,128)(2,1)} %copy.33), calls=%async_computation | async-start | bytes 2097152 | tf_op jit(solution)/shard_map/all_to_all | solution.py:138
  30.4 2.4 gather_fusion.1
  33.2 51.5 %all-to-all-done = bf16[80,4,8,128]{0,2,1,3:T(8,128)(2,1)S(1)} async-done(((bf16[80,4,8,128]{0,2,1,3:T(8,128)(2,1)}), bf16[80,4,8,128]{0,2,1,3:T(8,128)(2,1)S(1)}, u32[]{:S(2)}, u32[]{:S(2)}) %all-to-all-start) | async-done | bytes 655392 | tf_op jit(solution)/shard_map/all_to_all | solution.py:138
  86.0 0.9 broadcast_in_dim.1302
  86.9 4.0 all-to-all-start.1
  90.9 8.1 all-to-all-done.1
  99.2 0.7 gather_fusion
  100.0 0.8 select_select_fusion
  100.9 2.4 gather_fusion.2
  103.4 2.4 gather_fusion.3
  107.2 1.9 abs_convert_fusion.1
  110.0 0.7 copy-done.4
  110.8 1.6 convert_subtract_fusion
  112.4 141.9 %all-gather.2.cloned.1.call-done = f32[128,80,4,64]{1,3,2,0:T(8,128)} async-done(((f32[1,80,4,64]{1,3,2,0:T(8,128)}), f32[128,80,4,64]{1,3,2,0:T(8,128)}) %all-gather.2.cloned.1.call-update) | async-done | bytes 10485776 | tf_op jit(solution)/shard_map/all_gather | solution.py:24
  254.3 7.5 reduce_sum.5013
  262.1 325.8 %while.64 = (s32[]{:T(128)}, f32[5,80,80]{2,1,0:T(8,128)S(1)}, f32[5,80]{1,0:T(8,128)S(1)}, f32[80,64]{0,1:T(8,128)S(1)}, f32[64]{0:T(128)S(1)}, /*index=5*/f32[...) while((s32[]{:T(128)}, f32[5,80,80]{2,1,0:T(8,128)S(1)}, ...), condition=%wide.region_100.102_spmd.clone, body=%wide.region_4.101_spmd.clone.sunk | while | flops 50354160 | bytes 2492590 | solution.py:120
  265.7 0.7 fusion.2376
  267.8 0.7 fusion.2380
  326.8 0.7 fusion.2414
  328.4 0.7 fusion.2418
  430.5 0.7 fusion.2380
  489.4 0.7 fusion.2414
  491.1 0.7 fusion.2418
  587.9 325.4 %while.61 = (s32[]{:T(128)}, f32[5,80,80]{2,1,0:T(8,128)S(1)}, f32[5,80]{1,0:T(8,128)S(1)}, f32[80,64]{0,1:T(8,128)S(1)}, f32[64]{0:T(128)S(1)}, /*index=5*/f32[...) while((s32[]{:T(128)}, f32[5,80,80]{2,1,0:T(8,128)S(1)}, ...), condition=%wide.region_198.200_spmd, body=%wide.region_102.199_spmd.sunk | while | flops 50353360 | bytes 2489379 | solution.py:120
  593.3 0.7 fusion.1876
  652.2 0.7 fusion.1910
  653.9 0.7 fusion.1914
  753.8 0.7 fusion.1872
  755.9 0.7 fusion.1876
  814.8 0.7 fusion.1910
  816.5 0.7 fusion.1914
  913.4 325.5 %while.62 = (s32[]{:T(128)}, f32[5,80,80]{2,1,0:T(8,128)S(1)}, f32[5,80]{1,0:T(8,128)S(1)}, f32[80,64]{0,1:T(8,128)S(1)}, f32[64]{0:T(128)S(1)}, /*index=5*/f32[...) while((s32[]{:T(128)}, f32[5,80,80]{2,1,0:T(8,128)S(1)}, ...), condition=%wide.region_296.298_spmd, body=%wide.region_200.297_spmd.sunk | while | flops 50353360 | bytes 2489379 | solution.py:120
  918.8 0.7 fusion.2044
  977.7 0.7 fusion.2078
  979.3 0.7 fusion.2082
  1081.4 0.7 fusion.2044
  1140.3 0.7 fusion.2078
  1141.9 0.7 fusion.2082
  1238.8 325.5 %while.63 = (s32[]{:T(128)}, f32[5,80,80]{2,1,0:T(8,128)S(1)}, f32[5,80]{1,0:T(8,128)S(1)}, f32[80,64]{0,1:T(8,128)S(1)}, f32[64]{0:T(128)S(1)}, /*index=5*/f32[...) while((s32[]{:T(128)}, f32[5,80,80]{2,1,0:T(8,128)S(1)}, ...), condition=%wide.region_394.396_spmd, body=%wide.region_298.395_spmd.sunk | while | flops 50353360 | bytes 2489379 | solution.py:120
  1244.3 0.7 fusion.2212
  1303.2 0.7 fusion.2246
  1304.8 0.7 fusion.2250
  1406.9 0.7 fusion.2212
  1465.8 0.7 fusion.2246
  1467.4 0.7 fusion.2250
  1564.4 2.3 fusion.888
  1566.7 1.3 convert_element_type.110
  (1789 shorter events, 474.0 us)
Async XLA Ops:
  6.5 78.6 %copy-start = (f32[8,4]{0,1:T(4,128)S(1)}, f32[8,4]{0,1:T(4,128)}, u32[]{:S(2)}) copy-start(f32[8,4]{0,1:T(4,128)} %param.21) | copy-start | bytes 388
  6.5 23.7 %copy-start.6 = (s32[4,64]{1,0:T(4,128)S(1)}, s32[4,64]{1,0:T(4,128)}, u32[]{:S(2)}) copy-start(s32[4,64]{1,0:T(4,128)} %param.25) | copy-start | bytes 3076
  6.5 23.8 %copy-start.1 = (s32[4,64]{1,0:T(4,128)S(1)}, s32[4,64]{1,0:T(4,128)}, u32[]{:S(2)}) copy-start(s32[4,64]{1,0:T(4,128)} %param.24) | copy-start | bytes 3076
  9.6 23.4 %copy-start.8 = (f32[4]{0:T(128)S(1)}, f32[4]{0:T(128)}, u32[]{:S(2)}) copy-start(f32[4]{0:T(128)} %param.22) | copy-start | bytes 52
  9.6 23.4 %copy-start.9 = (f32[4]{0:T(128)S(1)}, f32[4]{0:T(128)}, u32[]{:S(2)}) copy-start(f32[4]{0:T(128)} %param.23) | copy-start | bytes 52
  9.6 75.1 %all-to-all-start = ((bf16[80,4,8,128]{0,2,1,3:T(8,128)(2,1)}), bf16[80,4,8,128]{0,2,1,3:T(8,128)(2,1)S(1)}, u32[]{:S(2)}, u32[]{:S(2)}) async-start(bf16[80,4,8,128]{0,2,1,3:T(8,128)(2,1)} %copy.33), calls=%async_computation | async-start | bytes 2097152 | tf_op jit(solution)/shard_map/all_to_all | solution.py:138
  85.2 5.8 copy-start.5
  85.9 14.8 copy-start.7
  86.0 14.9 copy-start.2
  86.9 12.2 all-to-all-start.1
  90.9 163.4 %all-gather.2.cloned.1.call-start = ((), (), s32[]{:S(2)}) async-start(), calls=%async_computation.2 | async-start | bytes 16908288 | tf_op jit(solution)/shard_map/all_gather | solution.py:24
  99.1 4.3 copy-start.3
  109.9 0.7 copy-start.4
Sparse Core Ops, SparseCore 0:
  100.9 153.3 all-gather.1
where the time goes:
time: 1590 us; the launch traced here: 1580 us
  loops' own time  814 us (51%)
  other arithmetic  387 us (24%)
  waiting for transfers between devices  201 us (13%)
  matrix products  88 us (6%)
  local copies, waits for them, and re-layouts  45.8 us (3%)
  starting transfers between devices  24.7 us (2%)
    another operation x4, loops' own time, run_batch(): lax.fori_loop(0, count_blocks, one_block, (transforms, offsets, jnp.zeros...  814 us
    reduce_sum x248, other arithmetic, serial_block(): center_col = jnp.mean(column)  159 us
    reduce_sum x248, other arithmetic, serial_block(): jnp.sum(anomaly_col * anomaly_col) / denominator + errors[column_id]  158 us
    all_gather x1, waiting for transfers between devices, over_pieces(): tiles = lax.all_gather(shard, axis)  142 us
    all_to_all x1, waiting for transfers between devices, body(): lax.all_to_all(background_members, 'region', split_axis=3, concat_axis=2,...  51.5 us
    dot_general x248, matrix products, serial_block(): jnp.dot(anomaly_col, anomaly_all, precision=highest) / denominator  49.4 us
    reduce_sum x240, other arithmetic, serial_block(): anomaly_all = current - jnp.mean(current, axis=0, keepdims=True)  43.4 us
  transfers between devices with their start and end apart: 3, of which 3 were waited for; matrix products, arithmetic and copies ran while one was open for 1% of the time, Pallas kernels for 0%

commit v1 on v0

v1 whole, which is shorter than its diff:
```python
import functools

import jax
import jax.numpy as jnp
from jax import lax
from jax.experimental import pallas as pl
from jax.experimental.pallas import tpu as pltpu
from jax.sharding import PartitionSpec as P

TILE = 32
STRIDE = 4
MEMBERS = 80
NOBS = 256
RING = 32
PLANE = 16
MESH = pl.DeviceIdType.MESH
highest = lax.Precision.HIGHEST


def reduce_kernel(part_ref, out_ref, own, recv1, recv2, s1, r1, s2, r2, s3, r3):
    region = lax.axis_index("region")
    lev = lax.axis_index("lev")
    yy = region // RING
    zc = lax.rem(region, RING)
    grp = lev * 4 + yy

    def ring_peer(o):
        return (yy * RING + lax.rem(zc + o, RING), lev)

    def group_peer(o):
        g = lax.rem(grp + o, PLANE)
        return (lax.rem(g, 4) * RING + zc, g // 4)

    barrier = pltpu.get_barrier_semaphore()

    @pl.loop(1, RING)
    def _(o):
        pl.semaphore_signal(barrier, inc=1, device_id=ring_peer(o), device_id_type=MESH)

    @pl.loop(1, PLANE)
    def _(o):
        pl.semaphore_signal(barrier, inc=1, device_id=group_peer(o), device_id_type=MESH)

    pl.semaphore_wait(barrier, RING + PLANE - 2)

    def copy1(o):
        row = pl.multiple_of(lax.rem(zc + o, RING) * 8, 8)
        return pltpu.make_async_remote_copy(
            src_ref=part_ref.at[pl.ds(row, 8)], dst_ref=recv1.at[o],
            send_sem=s1.at[o], recv_sem=r1.at[o],
            device_id=ring_peer(o), device_id_type=MESH)

    def copy2(o):
        return pltpu.make_async_remote_copy(
            src_ref=own.at[0], dst_ref=recv2.at[o],
            send_sem=s2.at[o], recv_sem=r2.at[o],
            device_id=group_peer(o), device_id_type=MESH)

    mine = pl.multiple_of(zc * 8, 8)

    def copy3(o):
        return pltpu.make_async_remote_copy(
            src_ref=own.at[1], dst_ref=out_ref.at[pl.ds(mine, 8)],
            send_sem=s3.at[o], recv_sem=r3.at[o],
            device_id=ring_peer(o), device_id_type=MESH)

    @pl.loop(1, RING)
    def _(o):
        copy1(o).start()

    def add1(o, total):
        copy1(o).wait_recv()
        return total + recv1[o]

    own[0] = lax.fori_loop(1, RING, add1, part_ref[pl.ds(mine, 8), :])

    @pl.loop(1, PLANE)
    def _(o):
        copy2(o).start()

    def add2(o, total):
        copy2(o).wait_recv()
        return total + recv2[o]

    own[1] = lax.fori_loop(1, PLANE, add2, own[0])

    @pl.loop(1, RING)
    def _(o):
        copy3(o).start()

    out_ref[pl.ds(mine, 8), :] = own[1]

    @pl.loop(1, RING)
    def _(o):
        copy3(o).wait_recv()

    @pl.loop(1, RING)
    def _(o):
        copy1(o).wait_send()
        copy3(o).wait_send()

    @pl.loop(1, PLANE)
    def _(o):
        copy2(o).wait_send()


def sum_everywhere(part):
    dma = pltpu.SemaphoreType.DMA
    return pl.pallas_call(
        reduce_kernel,
        out_shape=jax.ShapeDtypeStruct(part.shape, jnp.float32),
        in_specs=[pl.BlockSpec(memory_space=pltpu.VMEM)],
        out_specs=pl.BlockSpec(memory_space=pltpu.VMEM),
        scratch_shapes=[
            pltpu.VMEM((2, 8, 128), jnp.float32),
            pltpu.VMEM((RING, 8, 128), jnp.float32),
            pltpu.VMEM((PLANE, 8, 128), jnp.float32),
            dma((RING,)), dma((RING,)), dma((PLANE,)), dma((PLANE,)), dma((RING,)), dma((RING,)),
        ],
        compiler_params=pltpu.CompilerParams(collective_id=0, has_side_effects=True),
    )(part)


def column_sum(x):
    return jnp.sum(x, axis=0, keepdims=True)


def assimilate_all(priors, dist_ref, scal_ref):
    cols = priors.T[:MEMBERS]
    mean = column_sum(cols) / MEMBERS
    anomaly = cols - mean
    rows = lax.broadcasted_iota(jnp.int32, (MEMBERS, 128), 0)
    lanes = lax.broadcasted_iota(jnp.int32, (MEMBERS, 128), 1)
    transform = jnp.where(rows == lanes, 1.0, 0.0).astype(jnp.float32)
    offset = jnp.zeros((1, 128), jnp.float32)
    tiles = [anomaly[:, :128], anomaly[:, 128:], transform]
    means = [mean[:, :128], mean[:, 128:], offset]
    for half in range(2):
        for part in range(2):
            batch = half * 2 + part
            dist = [dist_ref[batch:batch + 1, h * 128:(h + 1) * 128] for h in range(half, 3)]

            def step(i, carry, part=part, batch=batch, dist=dist):
                tiles, means = carry
                where = jnp.full((MEMBERS, 128), part * 64 + i, jnp.int32)
                own = jnp.take_along_axis(tiles[0], where, axis=1)
                own_mean = jnp.take_along_axis(
                    jnp.broadcast_to(means[0], (8, 128)), where[:8], axis=1)[:1]
                t = batch * 64 + i
                noise = scal_ref[1, t]
                spread = column_sum(own * own) + noise
                root = lax.rsqrt(spread)
                gain = 1.0 / (spread + scal_ref[2, t] * (spread * root))
                innovation = (scal_ref[0, t] - own_mean) / spread
                inverse_cut = scal_ref[3, t]
                new_tiles, new_means = [], []
                for x, m, far in zip(tiles, means, dist):
                    cov = column_sum(x * own) * jnp.maximum(0.0, 1.0 - far * inverse_cut)
                    new_tiles.append(x - own * (cov * gain))
                    new_means.append(m + cov * innovation)
                return new_tiles, new_means

            tiles, means = lax.fori_loop(0, 64, step, (tiles, means))
        tiles, means = tiles[1:], means[1:]
    mixing = jnp.where(lanes < MEMBERS, tiles[0] + means[0], 0.0)
    rest = (1.0 - jnp.sum(mixing, axis=1, keepdims=True)) / MEMBERS
    return jnp.where(lanes < MEMBERS, mixing + rest, 0.0)


def solve_kernel(priors_ref, dist_ref, scal_ref, high_ref, low_ref):
    mixing = assimilate_all(priors_ref[...], dist_ref, scal_ref)
    high = mixing.astype(jnp.bfloat16)
    high_ref[...] = high
    low_ref[...] = (mixing - high.astype(jnp.float32)).astype(jnp.bfloat16)


def solve(priors, dist, scal):
    vmem = pl.BlockSpec(memory_space=pltpu.VMEM)
    shape = jax.ShapeDtypeStruct((MEMBERS, 128), jnp.bfloat16)
    return pl.pallas_call(
        solve_kernel,
        out_shape=(shape, shape),
        in_specs=[vmem, vmem, pl.BlockSpec(memory_space=pltpu.SMEM)],
        out_specs=(vmem, vmem),
        cost_estimate=pl.CostEstimate(flops=60_000_000, bytes_accessed=200_000_000, transcendentals=0),
    )(priors, dist, scal)


def body(
    background_members,
    channel_height_kernel,
    sensor_spread_down,
    sensor_spread_across,
    measurement_placement,
    measurement_ordering,
    group_area_number,
    taper_radius_limit,
    measured_amounts,
    measurement_noise_spread,
):
    region = lax.axis_index("region")
    members = background_members.shape[0]
    levels = background_members.shape[1]
    state = lax.all_to_all(background_members, "region", split_axis=3, concat_axis=2, tiled=True)[:, :, :, 0]

    order = measurement_ordering[:, :, None] == jnp.arange(64, dtype=jnp.int32)

    def ordered(a):
        return jnp.sum(jnp.where(order, a[:, None, :], 0), axis=2)

    picked = ordered(measurement_placement)
    values = ordered(measured_amounts)
    noise = ordered(measurement_noise_spread) * 79.0
    channel = picked // 64
    in_channel = channel[:, :, None] == jnp.arange(8, dtype=jnp.int32)
    cut = jnp.sum(jnp.where(in_channel, taper_radius_limit, 0), axis=2).astype(jnp.float32)
    scal = jnp.stack([values, noise, jnp.sqrt(noise), 1.0 / (cut + 1.0)]).reshape(4, NOBS)

    lane_region = jnp.concatenate([jnp.repeat(group_area_number, 64), jnp.full((128,), 1, jnp.int32) * region])
    dist = jnp.abs(lane_region[None] - group_area_number[:, None]).astype(jnp.float32)

    height = jnp.sum(jnp.where(in_channel[:, :, :, None], channel_height_kernel, 0.0), axis=2)
    row = region // 4
    column = (region % 4) * 8 + jnp.arange(8, dtype=jnp.int32)
    down = jnp.sum(jnp.where(jnp.arange(4) == row % 4, sensor_spread_down, 0.0))
    across = jnp.tile(sensor_spread_across, 2)
    site = picked % 64
    hit = (site[:, :, None] // 8 == row // 4) & (site[:, :, None] % 8 == column // 4)
    foot = jnp.where(hit, down * across, 0.0)
    weights = height[:, :, :, None] * foot[:, :, None, :]
    chosen = (group_area_number[:, None] == jnp.arange(128, dtype=jnp.int32)).astype(jnp.bfloat16)
    seen = jnp.einsum("mlpr,kr->klpm", background_members, chosen, preferred_element_type=jnp.float32)
    part = jnp.einsum("ktlp,klpm->ktm", weights, seen, precision=highest).reshape(NOBS, members)
    priors = sum_everywhere(jnp.pad(part, ((0, 0), (0, 128 - members))))
    high, low = solve(priors, dist, scal)
    flat = state.reshape(members, levels * 1024)
    result = jnp.dot(high[:, :members], flat, preferred_element_type=jnp.float32) + jnp.dot(
        low[:, :members], flat, preferred_element_type=jnp.float32)
    return result.astype(jnp.bfloat16).reshape(members, levels, 1, 1024)


def solution(mesh):
    return jax.shard_map(
        body,
        mesh=mesh,
        in_specs=(P(None, "lev", "region", None), P(None, "lev"), P(), P(), P(), P(), P(), P(), P(), P()),
        out_specs=P(None, "lev", "region", None),
        check_vma=False,
    )
```

time: 1590 us -> 137 us (0.09)
  loops' own time: 814 us -> 0 us
  other arithmetic: 387 us -> 3.3 us
  waiting for transfers between devices: 201 us -> 0.01 us
  Pallas kernels: 0 us -> 105 us
  matrix products: 88 us -> 1.94 us
  local copies, waits for them, and re-layouts: 45.8 us -> 6.22 us
    another operation x4 -> x0, loops' own time: 814 us -> none  [run_batch(): lax.fori_loop(0, count_blocks, one_block, (transforms, offsets, jnp.zeros...]
    reduce_sum x757 -> x5, other arithmetic: 371 us -> 1.25 us  [the longest x1 0.6 us: body(): down = jnp.sum(jnp.where(jnp.arange(4) == row % 4, sensor_spread_down, 0.0))]
    all_gather x1 -> x0, waiting for transfers between devices: 142 us -> none  [over_pieces(): tiles = lax.all_gather(shard, axis)]
    pallas_call x0 -> x2, Pallas kernels: none -> 105 us  [the longest x1 72.3 us: sum_everywhere(): pl.pallas_call(reduce_kernel, out_shape=jax.ShapeDtypeStruct(part.shape,...]
    dot_general x386 -> x4, matrix products: 88 us -> 1.94 us  [the longest x1 0.54 us: body(): jnp.einsum('mlpr,kr->klpm', background_members, chosen, preferred_element...]
    all_to_all x1, waiting for transfers between devices: 51.5 us -> 0.01 us  [body(): lax.all_to_all(background_members, 'region', split_axis=3, concat_axis=2,...]
    slice x42 -> x0, local copies, waits for them, and re-layouts: 28.5 us -> none  [the longest x16 11.6 us: serial_block(): innovation = values[column_id] - center_col]
  transfers between devices with their start and end apart: 3 -> 1, of which waited for: 3 -> 0; matrix products, arithmetic and copies ran while one was open for 1% -> 4% of each run, Pallas kernels for 0% -> 76%
where the time goes in v1:
time: 137 us
  Pallas kernels  105 us (77%)
  starting transfers between devices  20.7 us (15%)
  local copies, waits for them, and re-layouts  6.22 us (5%)
  other arithmetic  3.3 us (2%)
  matrix products  1.94 us (1%)
    pallas_call x1, Pallas kernels, sum_everywhere(): pl.pallas_call(reduce_kernel, out_shape=jax.ShapeDtypeStruct(part.shape,...  72.3 us
    pallas_call x1, Pallas kernels, solve(): pl.pallas_call(solve_kernel, out_shape=(shape, shape), in_specs=[vmem, vm...  32.4 us
    all_to_all x1, starting transfers between devices, body(): lax.all_to_all(background_members, 'region', split_axis=3, concat_axis=2,...  20.7 us
    unnamed x25, local copies, waits for them, and re-layouts  3.55 us
  transfers between devices with their start and end apart: 1, of which 0 were waited for; matrix products, arithmetic and copies ran while one was open for 4% of the time, Pallas kernels for 76%

profile of v1, /device:TPU:1, one launch (start us, length us, event | category | flops | bytes accessed | tf_op | source)
XLA Modules:
  0.0 137.1 jit_solution(9326958779898079420)
XLA Ops:
  0.0 3.0 %copy.30 = bf16[80,4,8,128]{0,2,1,3:T(8,128)(2,1)} copy(bf16[80,4,8,128]{3,2,1,0:T(8,128)(2,1)} %param.10) | data formatting | bytes 1310720 | tf_op args[0]
  3.0 0.0 copy-start.10
  3.0 0.0 copy-start.11
  3.0 0.0 copy-start.5
  3.0 0.0 copy-start.9
  3.0 0.0 copy-start.6
  3.0 0.0 copy-start.7
  3.0 0.0 copy-start.8
  3.0 0.0 copy-start
  3.1 20.7 %all-to-all-start = ((bf16[80,4,8,128]{0,2,1,3:T(8,128)(2,1)}), bf16[80,4,8,128]{0,2,1,3:T(8,128)(2,1)S(1)}, u32[]{:S(2)}, u32[]{:S(2)}) async-start(bf16[80,4,8,128]{0,2,1,3:T(8,128)(2,1)} %copy.30), calls=%async_computation | async-start | bytes 2097152 | tf_op jit(solution)/shard_map/all_to_all | solution.py:204
  23.8 0.0 copy-done.10
  23.8 0.6 fusion.16
  24.4 0.0 copy-done.11
  24.4 0.6 broadcast_multiply_fusion.1
  25.1 0.1 mul.53
  25.2 0.0 copy-done.4
  25.2 0.1 broadcast_in_dim.94
  25.3 0.1 reshape.179
  25.3 0.0 copy-done.3
  25.3 0.0 copy-done.5
  25.3 0.2 select_reduce_fusion.2
  25.6 0.0 copy-done.9
  25.6 0.1 select_reduce_fusion.4
  25.7 0.1 div.84
  25.8 0.0 copy-done.6
  25.8 0.0 copy-done.7
  25.8 0.2 select_reduce_fusion.1
  26.0 0.1 stack.4
  26.1 0.1 mul.58
  26.3 0.0 copy-done.8
  26.3 0.1 select_reduce_fusion.3
  26.4 0.1 and_select_fusion
  26.5 0.0 copy-done
  26.5 0.5 convolution_bitcast_fusion
  27.0 0.4 fusion.2
  27.4 0.7 pad.5.part_ref
  28.1 72.3 %shard_map.100.priors_ref = f32[256,128]{1,0:T(8,128)} custom-call(f32[256,128]{1,0:T(8,128)} %pad.5.part_ref), custom_call_target="tpu_custom_call" | custom-call | tf_op jit(solution)/shard_map/pallas_call | solution.py:109
  100.4 0.6 pad_maximum_fusion.scal_ref
  101.0 0.7 abs_convert_fusion.dist_ref
  101.6 32.4 %shard_map.101 = (bf16[80,128]{1,0:T(8,128)(2,1)}, bf16[80,128]{1,0:T(8,128)(2,1)}) custom-call(f32[256,128]{1,0:T(8,128)} %shard_map.100.priors_ref, f32[4,384]{1,0:T(4,128)} %abs_convert_fusion.dist_ref, f32[4,256]{1,0:T(4,128)} %pad_maximum_fusion.scal_ref), custom_call_target="tpu_custom_call" | custom-call | flops 60000000 | bytes 200000000 | tf_op jit(solution)/shard_map/pallas_call | solution.py:180
  134.1 0.0 all-to-all-done
  134.1 0.2 copy.31
  134.3 0.0 copy-start.1
  134.3 0.5 copy-done.2
  134.8 0.5 fusion.8
  135.3 0.0 copy-done.1
  135.3 0.5 fusion
  135.8 1.3 reshape.180
  (12 shorter events, 0.1 us)
Async XLA Ops:
  3.0 20.8 %copy-start.10 = (f32[4]{0:T(128)S(1)}, f32[4]{0:T(128)}, u32[]{:S(2)}) copy-start(f32[4]{0:T(128)} %param.12) | copy-start | bytes 52
  3.0 21.5 %copy-start.11 = (f32[4]{0:T(128)S(1)}, f32[4]{0:T(128)}, u32[]{:S(2)}) copy-start(f32[4]{0:T(128)} %param.13) | copy-start | bytes 52
  3.0 22.2 %copy-start.4 = (s32[4]{0:T(128)S(1)}, s32[4]{0:T(128)}, u32[]{:S(2)}) copy-start(s32[4]{0:T(128)} %param.16) | copy-start | bytes 52
  3.0 22.4 %copy-start.3 = (s32[4,64]{1,0:T(4,128)S(1)}, s32[4,64]{1,0:T(4,128)}, u32[]{:S(2)}) copy-start(s32[4,64]{1,0:T(4,128)} %param.15) | copy-start | bytes 3076
  3.0 22.4 %copy-start.5 = (s32[4,64]{1,0:T(4,128)S(1)}, s32[4,64]{1,0:T(4,128)}, u32[]{:S(2)}) copy-start(s32[4,64]{1,0:T(4,128)} %param.14) | copy-start | bytes 3076
  3.0 22.6 %copy-start.9 = (s32[8]{0:T(128)S(1)}, s32[8]{0:T(128)}, u32[]{:S(2)}) copy-start(s32[8]{0:T(128)} %param.17) | copy-start | bytes 100
  3.0 22.8 %copy-start.6 = (f32[4,64]{1,0:T(4,128)S(1)}, f32[4,64]{1,0:T(4,128)}, u32[]{:S(2)}) copy-start(f32[4,64]{1,0:T(4,128)} %param.18) | copy-start | bytes 3076
  3.0 22.8 %copy-start.7 = (f32[4,64]{1,0:T(4,128)S(1)}, f32[4,64]{1,0:T(4,128)}, u32[]{:S(2)}) copy-start(f32[4,64]{1,0:T(4,128)} %param.19) | copy-start | bytes 3076
  3.0 23.2 %copy-start.8 = (f32[8,4]{0,1:T(4,128)S(1)}, f32[8,4]{0,1:T(4,128)}, u32[]{:S(2)}) copy-start(f32[8,4]{0,1:T(4,128)} %param.11) | copy-start | bytes 388
  3.0 23.4 %copy-start = (bf16[80,4,8,128]{3,2,1,0:T(8,128)(2,1)S(1)}, bf16[80,4,8,128]{3,2,1,0:T(8,128)(2,1)}, u32[]{:S(2)}) copy-start(bf16[80,4,8,128]{3,2,1,0:T(8,128)(2,1)} %param.10) | copy-start | bytes 1966084
  3.1 131.0 %all-to-all-start = ((bf16[80,4,8,128]{0,2,1,3:T(8,128)(2,1)}), bf16[80,4,8,128]{0,2,1,3:T(8,128)(2,1)S(1)}, u32[]{:S(2)}, u32[]{:S(2)}) async-start(bf16[80,4,8,128]{0,2,1,3:T(8,128)(2,1)} %copy.30), calls=%async_computation | async-start | bytes 2097152 | tf_op jit(solution)/shard_map/all_to_all | solution.py:204
  134.1 0.7 copy-start.2
  134.3 1.0 copy-start.1

commit v2 on v1

v2 whole, which is shorter than its diff:
```python
import jax
import jax.numpy as jnp
from jax import lax
from jax.experimental import pallas as pl
from jax.experimental.pallas import tpu as pltpu
from jax.sharding import PartitionSpec as P

MEMBERS = 80
NOBS = 256
BATCH = 64
CHUNK = 16
RING = 32
MESH = pl.DeviceIdType.MESH
highest = lax.Precision.HIGHEST
f32 = jnp.float32
bf16 = jnp.bfloat16


def column_sum(x):
    return jnp.sum(x, axis=0, keepdims=True)


def roll(x, shift):
    return pltpu.roll(x, shift % 128, 1)


def exchange(low, high, bit, lanes):
    keep = (lanes // (1 << bit)) % 2 == 0
    return (
        jnp.where(keep, low, roll(high, 1 << bit)),
        jnp.where(keep, roll(low, -(1 << bit)), high),
    )


def exchange_four(tiles, bit, lanes):
    a, b, c, d = tiles
    a, b = exchange(a, b, bit, lanes)
    c, d = exchange(c, d, bit, lanes)
    a, c = exchange(a, c, bit + 1, lanes)
    b, d = exchange(b, d, bit + 1, lanes)
    return a, b, c, d


def step_terms(own, own_mean, value, noise, root_noise):
    spread = column_sum(own * own) + noise
    root = lax.rsqrt(spread)
    gain = 1.0 / (spread + root_noise * (spread * root))
    return gain, (value - own_mean) / spread


def kernel(
    x_ref, table_ref, group_ref, out_ref,
    flat, tiles_f, tiles_b, recv_z, turned, recv_y,
    part, total, recv1, recv2, priors, terms,
    s1, r1, s2, r2, s3, r3, sz, rz, sy, ry,
):
    region = lax.axis_index("region")
    lev = lax.axis_index("lev")
    yy = region // RING
    zc = lax.rem(region, RING)
    z = zc // 2
    core = lax.rem(zc, 2)
    slab = lev * 8 + yy * 2 + core

    def slab_peer(o):
        g = lax.rem(slab + o, 32)
        return (lax.rem(g // 2, 4) * RING + z * 2 + lax.rem(g, 2), g // 8)

    def far_z(h):
        e = h // 2
        size = e // 2 + 1
        dz = size + lax.rem(e, 2) * (16 - 2 * size)
        return lax.rem(z + dz, 16) * 2 + lax.rem(h, 2)

    def at_ring(other):
        return (yy * RING + other, lev)

    def line_peer(o):
        return (yy * RING + lax.rem(z + o, 16) * 2 + core, lev)

    def y_peer(o):
        return (lax.rem(yy + o, 4) * RING + zc, lev)

    barrier = pltpu.get_barrier_semaphore()

    @pl.loop(1, 32)
    def _(o):
        pl.semaphore_signal(barrier, inc=1, device_id=slab_peer(o), device_id_type=MESH)

    @pl.loop(0, 30)
    def _(h):
        pl.semaphore_signal(barrier, inc=1, device_id=at_ring(far_z(h)), device_id_type=MESH)

    lanes = lax.broadcasted_iota(jnp.int32, (MEMBERS, 128), 1)

    flat[...] = x_ref[...].astype(f32).reshape(MEMBERS * 32, 128)
    swapped = ((lanes // 8) % 4) * 32 + (lanes // 32) * 8 + lanes % 8

    @pl.loop(0, 32)
    def _(i):
        tiles_f[i] = jnp.take_along_axis(flat[pl.ds(i, MEMBERS, stride=32), :], swapped, axis=1)

    for tile_bit, lane_bit in ((0, 0), (1, 1), (2, 2), (3, 5), (4, 6)):
        size = 1 << tile_bit

        @pl.loop(0, 16)
        def _(q, size=size, lane_bit=lane_bit):
            low = (q // size) * (2 * size) + lax.rem(q, size)
            a, b = exchange(tiles_f[low], tiles_f[low + size], lane_bit, lanes)
            tiles_f[low] = a
            tiles_f[low + size] = b

    @pl.loop(0, 32)
    def _(i):
        tiles_b[i] = tiles_f[i].astype(bf16)

    table = table_ref[...]
    turned_table = table.T
    wide = lax.broadcasted_iota(jnp.int32, (BATCH, 128), 1)
    wide_f = wide.astype(f32)
    row_block = (region // 16).astype(f32)
    lane_column = (lax.rem(region, 4) * 2 + (wide % 8) // 4).astype(f32)
    lane_y = (wide // 8) % 4
    part[...] = jnp.zeros_like(part)
    for k in range(4):
        place = group_ref[k]
        order = turned_table[:BATCH, 4 + k:5 + k] == wide_f

        def ordered(row, order=order):
            return jnp.sum(jnp.where(order, table[row:row + 1], 0.0), axis=1, keepdims=True)

        picked = ordered(k)
        value = ordered(8 + k)
        noise = ordered(12 + k) * 79.0
        channel = jnp.floor(picked * (1.0 / 64.0))
        site = picked - channel * 64.0
        down = jnp.floor(site * 0.125)
        along = site - down * 8.0
        cut = jnp.sum(jnp.where(channel == wide_f, table[16:17], 0.0), axis=1, keepdims=True)
        height = jnp.zeros((BATCH, 128), f32)
        for c in range(8):
            height = jnp.where(channel == float(c), table[24 + c:25 + c], height)
        hit = (down == row_block) & (along == lane_column) & (lane_y == place // RING)
        weights = jnp.where(hit, height * table[17:18], 0.0)
        rows = pl.ds(k * BATCH, BATCH)
        part[rows, :MEMBERS] = lax.dot_general(
            weights, tiles_f[lax.rem(place, RING)], (((1,), (1,)), ((), ())),
            precision=highest, preferred_element_type=f32)
        terms[0, rows, :] = jnp.broadcast_to(value, (BATCH, 128))
        terms[1, rows, :] = jnp.broadcast_to(noise, (BATCH, 128))
        terms[2, rows, :] = jnp.broadcast_to(jnp.sqrt(noise), (BATCH, 128))
        terms[3, rows, :] = jnp.broadcast_to(1.0 / (cut + 1.0), (BATCH, 128))

    pl.semaphore_wait(barrier, 61)

    def copy1(o):
        row = pl.multiple_of(lax.rem(slab + o, 32) * 8, 8)
        return pltpu.make_async_remote_copy(
            src_ref=part.at[pl.ds(row, 8)], dst_ref=recv1.at[o],
            send_sem=s1.at[o], recv_sem=r1.at[o], device_id=slab_peer(o), device_id_type=MESH)

    def copy2(o):
        return pltpu.make_async_remote_copy(
            src_ref=total.at[0], dst_ref=recv2.at[o],
            send_sem=s2.at[o], recv_sem=r2.at[o], device_id=line_peer(o), device_id_type=MESH)

    mine = pl.multiple_of(slab * 8, 8)

    def copy3(o):
        return pltpu.make_async_remote_copy(
            src_ref=total.at[1], dst_ref=priors.at[pl.ds(mine, 8)],
            send_sem=s3.at[o], recv_sem=r3.at[o], device_id=slab_peer(o), device_id_type=MESH)

    def copy_z(other):
        return pltpu.make_async_remote_copy(
            src_ref=tiles_b.at[other], dst_ref=recv_z.at[zc],
            send_sem=sz.at[other], recv_sem=rz.at[zc], device_id=at_ring(other), device_id_type=MESH)

    def arrived_z(other):
        pltpu.make_async_remote_copy(
            src_ref=tiles_b.at[other], dst_ref=recv_z.at[other],
            send_sem=sz.at[other], recv_sem=rz.at[other], device_id=at_ring(other), device_id_type=MESH).wait_recv()

    def copy_y(block, o):
        to = lax.rem(yy + o, 4)
        return pltpu.make_async_remote_copy(
            src_ref=turned.at[block, to], dst_ref=recv_y.at[yy, block],
            send_sem=sy.at[block, o], recv_sem=ry.at[block, o], device_id=y_peer(o), device_id_type=MESH)

    @pl.loop(1, 32)
    def _(o):
        copy1(o).start()

    copy_z(z * 2 + 1 - core).start()

    @pl.loop(0, 12)
    def _(h):
        copy_z(far_z(h)).start()

    def add1(o, acc):
        copy1(o).wait_recv()
        return acc + recv1[o]

    total[0] = lax.fori_loop(1, 32, add1, part[pl.ds(mine, 8), :])

    @pl.loop(1, 16)
    def _(o):
        copy2(o).start()

    @pl.loop(12, 30)
    def _(h):
        copy_z(far_z(h)).start()

    recv_z[zc] = tiles_b[zc]

    def add2(o, acc):
        copy2(o).wait_recv()
        return acc + recv2[o]

    total[1] = lax.fori_loop(1, 16, add2, total[0])

    @pl.loop(1, 32)
    def _(o):
        copy3(o).start()

    priors[pl.ds(mine, 8), :] = total[1]

    @pl.loop(1, 32)
    def _(o):
        copy3(o).wait_recv()

    def forward(e):
        away = (e + 1) // 2
        block = lax.rem(z // 2 + (away if e % 2 else 8 - away), 8)
        if e == 0:
            @pl.loop(1, 4)
            def _(u):
                arrived_z(block * 4 + lax.rem(zc + u, 4))
        else:
            @pl.loop(0, 4)
            def _(u):
                arrived_z(block * 4 + u)
        four = [recv_z[block * 4 + j].astype(f32) for j in range(4)]
        four = exchange_four(four, 3, lanes)
        for j in range(4):
            turned[block, j] = four[j].astype(bf16)

        @pl.loop(1, 4)
        def _(o):
            copy_y(block, o).start()

        recv_y[yy, block] = turned[block, yy]

    cols = priors[...].T[:MEMBERS]
    mean = column_sum(cols) / MEMBERS
    anomaly = cols - mean
    members = lax.broadcasted_iota(jnp.int32, (MEMBERS, 128), 0)
    tiles = [anomaly[:, :128], anomaly[:, 128:], jnp.where(members == lanes, 1.0, 0.0).astype(f32)]
    means = [mean[:, :128], mean[:, 128:], jnp.zeros((1, 128), f32)]
    lane_row = lanes[:1]
    for batch in range(4):
        here = group_ref[batch]

        def away_from(other, here=here):
            return jnp.full((1, 128), jnp.abs(other - here), jnp.int32).astype(f32)

        if batch % 2 == 0:
            far = [jnp.where(lane_row < BATCH, 0.0, away_from(group_ref[batch + 1]))]
        else:
            far = [jnp.zeros((1, 128), f32)]
        if batch < 2:
            far.append(jnp.where(lane_row < BATCH, away_from(group_ref[2]), away_from(group_ref[3])))
        far.append(away_from(region))

        def chunk(c, carry, batch=batch, fixed=far[1:]):
            tiles, means, near = carry
            start = pl.multiple_of(batch * BATCH + c * CHUNK, CHUNK)
            block = [terms[i, pl.ds(start, CHUNK), :] for i in range(4)]
            for u in range(CHUNK):
                value, noise, root_noise, inverse_cut = [b[u:u + 1] for b in block]
                own = jnp.broadcast_to(tiles[0][:, u:u + 1], (MEMBERS, 128))
                own_mean = jnp.broadcast_to(means[0][:, u:u + 1], (1, 128))
                gain, innovation = step_terms(own, own_mean, value, noise, root_noise)
                new_tiles, new_means = [], []
                for x, m, distance in zip(tiles, means, [near] + fixed):
                    cov = column_sum(x * own) * jnp.maximum(0.0, 1.0 - distance * inverse_cut)
                    new_tiles.append(x - own * (cov * gain))
                    new_means.append(m + cov * innovation)
                tiles, means = new_tiles, new_means
            tiles = [roll(tiles[0], -CHUNK)] + tiles[1:]
            means = [roll(means[0], -CHUNK)] + means[1:]
            return tiles, means, roll(near, -CHUNK)

        tiles, means, _ = lax.fori_loop(0, BATCH // CHUNK, chunk, (tiles, means, far[0]))
        if batch % 2 == 1:
            tiles, means = tiles[1:], means[1:]
        forward(2 * batch)
        forward(2 * batch + 1)

    mixing = jnp.where(lanes < MEMBERS, tiles[0] + means[0], 0.0)
    rest = (1.0 - jnp.sum(mixing, axis=1, keepdims=True)) / MEMBERS
    mixing = (mixing + rest)[:, :MEMBERS]
    high = mixing.astype(bf16)
    low = (mixing - high.astype(f32)).astype(bf16)

    @pl.loop(0, 8)
    def _(block):
        @pl.loop(1, 4)
        def _(o):
            copy_y(block, o).wait_recv()

    @pl.loop(0, 8)
    def _(i):
        source = i // 2
        half = lax.rem(i, 2)
        four = []
        for j in range(4):
            block = recv_y[source, half * 4 + j]
            four.append(
                jnp.dot(high, block, preferred_element_type=f32)
                + jnp.dot(low, block, preferred_element_type=f32))
        four = exchange_four(four, 5, lanes)
        for level in range(4):
            out_ref[level, :, pl.ds(pl.multiple_of(i * 128, 128), 128)] = four[level].astype(bf16)

    copy_z(z * 2 + 1 - core).wait_send()

    @pl.loop(0, 30)
    def _(h):
        copy_z(far_z(h)).wait_send()

    @pl.loop(1, 32)
    def _(o):
        copy1(o).wait_send()
        copy3(o).wait_send()

    @pl.loop(1, 16)
    def _(o):
        copy2(o).wait_send()

    @pl.loop(0, 8)
    def _(block):
        @pl.loop(1, 4)
        def _(o):
            copy_y(block, o).wait_send()


def body(
    background_members,
    channel_height_kernel,
    sensor_spread_down,
    sensor_spread_across,
    measurement_placement,
    measurement_ordering,
    group_area_number,
    taper_radius_limit,
    measured_amounts,
    measurement_noise_spread,
):
    row = lax.axis_index("region") // 4
    down = jnp.sum(jnp.where(jnp.arange(4) == row % 4, sensor_spread_down, 0.0))

    def widen(a):
        return jnp.pad(a.astype(f32), ((0, 0), (0, 128 - a.shape[1])))

    table = jnp.concatenate([
        widen(measurement_placement), widen(measurement_ordering),
        widen(measured_amounts), widen(measurement_noise_spread),
        widen(taper_radius_limit[None]), jnp.tile(sensor_spread_across * down, 32)[None],
        jnp.zeros((6, 128), f32), jnp.repeat(channel_height_kernel, 32, axis=1)])
    vmem = pl.BlockSpec(memory_space=pltpu.VMEM)
    dma = pltpu.SemaphoreType.DMA
    result = pl.pallas_call(
        kernel,
        out_shape=jax.ShapeDtypeStruct((4, MEMBERS, 1024), bf16),
        in_specs=[vmem, vmem, pl.BlockSpec(memory_space=pltpu.SMEM)],
        out_specs=vmem,
        scratch_shapes=[
            pltpu.VMEM((MEMBERS * 32, 128), f32),
            pltpu.VMEM((32, MEMBERS, 128), f32),
            pltpu.VMEM((32, MEMBERS, 128), bf16),
            pltpu.VMEM((32, MEMBERS, 128), bf16),
            pltpu.VMEM((8, 4, MEMBERS, 128), bf16),
            pltpu.VMEM((4, 8, MEMBERS, 128), bf16),
            pltpu.VMEM((NOBS, 128), f32),
            pltpu.VMEM((2, 8, 128), f32),
            pltpu.VMEM((32, 8, 128), f32),
            pltpu.VMEM((16, 8, 128), f32),
            pltpu.VMEM((NOBS, 128), f32),
            pltpu.VMEM((4, NOBS, 128), f32),
            dma((32,)), dma((32,)), dma((16,)), dma((16,)), dma((32,)), dma((32,)),
            dma((32,)), dma((32,)), dma((8, 4)), dma((8, 4)),
        ],
        compiler_params=pltpu.CompilerParams(
            collective_id=0, has_side_effects=True, vmem_limit_bytes=32 * 1024 * 1024),
    )(background_members, table, group_area_number)
    return jnp.transpose(result, (1, 0, 2))[:, :, None, :]


def solution(mesh):
    return jax.shard_map(
        body,
        mesh=mesh,
        in_specs=(P(None, "lev", "region", None), P(None, "lev"), P(), P(), P(), P(), P(), P(), P(), P()),
        out_specs=P(None, "lev", "region", None),
        check_vma=False,
    )
```

time: 137 us -> 104 us (0.76)
  starting transfers between devices: 20.7 us -> 0 us
  Pallas kernels: 105 us -> 94.6 us
  other arithmetic: 3.3 us -> 1.27 us
  matrix products: 1.94 us -> 0 us
    all_to_all x1 -> x0, starting transfers between devices: 20.7 us -> none  [body(): lax.all_to_all(background_members, 'region', split_axis=3, concat_axis=2,...]
    pallas_call x2 -> x1, Pallas kernels: 105 us -> 94.6 us  [body(): pl.pallas_call(kernel, out_shape=jax.ShapeDtypeStruct((4, MEMBERS, 1024),...]
    unnamed x25 -> x21, local copies, waits for them, and re-layouts: 3.55 us -> 5.82 us
    dot_general x4 -> x0, matrix products: 1.94 us -> none  [the longest x1 0.54 us: body(): jnp.einsum('mlpr,kr->klpm', background_members, chosen, preferred_element...]
  transfers between devices with their start and end apart: 1 -> 0, of which waited for: 0 -> 0; matrix products, arithmetic and copies ran while one was open for 4% -> 0% of each run, Pallas kernels for 76% -> 0%
where the time goes in v2:
time: 104 us
  Pallas kernels  94.6 us (91%)
  local copies, waits for them, and re-layouts  7.53 us (7%)
  other arithmetic  1.27 us (1%)
    pallas_call x1, Pallas kernels, body(): pl.pallas_call(kernel, out_shape=jax.ShapeDtypeStruct((4, MEMBERS, 1024),...  94.6 us
    unnamed x21, local copies, waits for them, and re-layouts  5.82 us

profile of v2, /device:TPU:1, one launch (start us, length us, event | category | flops | bytes accessed | tf_op | source)
XLA Modules:
  0.0 103.5 jit_solution(5878064493526285453)
XLA Ops:
  0.0 0.0 copy-start.7
  0.0 0.7 copy-done.7
  0.7 0.0 copy-start.8
  0.7 0.6 fusion
  1.3 0.1 copy-done.8
  1.3 0.0 copy-start.9
  1.3 0.7 broadcast_multiply_fusion
  2.0 0.0 copy-done.9
  2.0 0.0 copy-start.3
  2.0 0.6 copy-done.3
  2.7 0.0 copy-start.4
  2.7 0.7 copy-done.4
  3.4 0.0 copy-start.5
  3.4 0.7 copy-done.5
  4.0 0.0 copy-start.6
  4.1 0.7 copy-done.6
  4.7 0.0 copy-start.2
  4.7 0.7 copy-done.2
  5.4 0.1 copy.13
  5.5 0.1 broadcast_in_dim.16
  5.6 0.1 reshape.5
  5.7 0.1 broadcast_in_dim_tile.3
  5.8 0.0 copy-start.1
  5.8 0.1 concatenate.3.table_ref
  5.9 0.6 copy-done.1
  6.4 0.0 copy-start
  6.4 1.1 %copy-done = bf16[80,4,8,128]{3,2,1,0:T(8,128)(2,1)S(1)} copy-done((bf16[80,4,8,128]{3,2,1,0:T(8,128)(2,1)S(1)}, bf16[80,4,8,128]{3,2,1,0:T(8,128)(2,1)}, u32[]{:S(2)}) %copy-start) | copy-done | bytes 655384
  7.5 94.6 %shard_map.100 = bf16[4,80,1024]{2,1,0:T(8,128)(2,1)S(1)} custom-call(bf16[80,4,8,128]{3,2,1,0:T(8,128)(2,1)S(1)} %copy-done, f32[32,128]{1,0:T(8,128)S(1)} %concatenate.3.table_ref, s32[4]{0:T(128)S(1)} %copy-done.1), custom_call_target="tpu_custom_call" | custom-call | tf_op jit(solution)/shard_map/pallas_call | solution.py:373
  102.2 1.3 %copy.14 = bf16[80,4,1,1024]{3,1,2,0:T(4,128)(2,1)} copy(bf16[80,4,1,1024]{3,0,1,2:T(8,128)(2,1)S(1)} %bitcast.5) | data formatting | bytes 1310720 | tf_op jit(solution)/shard_map/broadcast_in_dim | solution.py:397
  (10 shorter events, 0.0 us)
Async XLA Ops:
  0.0 0.7 copy-start.7
  0.7 0.7 copy-start.8
  1.3 0.7 copy-start.9
  2.0 0.7 copy-start.3
  2.7 0.7 copy-start.4
  3.4 0.7 copy-start.5
  4.0 0.7 copy-start.6
  4.7 0.7 copy-start.2
  5.8 0.7 copy-start.1
  6.4 1.1 %copy-start = (bf16[80,4,8,128]{3,2,1,0:T(8,128)(2,1)S(1)}, bf16[80,4,8,128]{3,2,1,0:T(8,128)(2,1)}, u32[]{:S(2)}) copy-start(bf16[80,4,8,128]{3,2,1,0:T(8,128)(2,1)} %x_ref.1) | copy-start | bytes 1966084

commit v3 on v2

--- a/solution.py
+++ b/solution.py
@@ -9,6 +9,7 @@
 NOBS = 256
 BATCH = 64
 CHUNK = 16
+AHEAD = 3
 RING = 32
 MESH = pl.DeviceIdType.MESH
 highest = lax.Precision.HIGHEST
@@ -41,16 +42,21 @@
     return a, b, c, d
 
 
+def across_lanes(x, lane):
+    return jnp.broadcast_to(x[:, lane:lane + 1], (x.shape[0], 128))
+
+
 def step_terms(own, own_mean, value, noise, root_noise):
     spread = column_sum(own * own) + noise
     root = lax.rsqrt(spread)
     gain = 1.0 / (spread + root_noise * (spread * root))
-    return gain, (value - own_mean) / spread
+    return gain, (value - own_mean) * (root * root)
 
 
 def kernel(
-    x_ref, table_ref, group_ref, out_ref,
-    flat, tiles_f, tiles_b, recv_z, turned, recv_y,
+    x_ref, place_ref, order_ref, value_ref, noise_ref,
+    height_ref, down_ref, across_ref, limit_ref, group_ref, out_ref,
+    table, flat, tiles_f, tiles_b, recv_z, turned, recv_y,
     part, total, recv1, recv2, priors, terms,
     s1, r1, s2, r2, s3, r3, sz, rz, sy, ry,
 ):
@@ -95,61 +101,92 @@
 
     flat[...] = x_ref[...].astype(f32).reshape(MEMBERS * 32, 128)
     swapped = ((lanes // 8) % 4) * 32 + (lanes // 32) * 8 + lanes % 8
-
-    @pl.loop(0, 32)
-    def _(i):
-        tiles_f[i] = jnp.take_along_axis(flat[pl.ds(i, MEMBERS, stride=32), :], swapped, axis=1)
-
-    for tile_bit, lane_bit in ((0, 0), (1, 1), (2, 2), (3, 5), (4, 6)):
-        size = 1 << tile_bit
-
-        @pl.loop(0, 16)
-        def _(q, size=size, lane_bit=lane_bit):
-            low = (q // size) * (2 * size) + lax.rem(q, size)
-            a, b = exchange(tiles_f[low], tiles_f[low + size], lane_bit, lanes)
-            tiles_f[low] = a
-            tiles_f[low + size] = b
-
-    @pl.loop(0, 32)
-    def _(i):
-        tiles_b[i] = tiles_f[i].astype(bf16)
-
-    table = table_ref[...]
-    turned_table = table.T
+    wanted = jnp.full((MEMBERS, 128), group_ref[0], jnp.int32)
+    for k in range(1, 4):
+        wanted = jnp.where(lanes // 32 == k, group_ref[k], wanted)
+
+    def first_pass(q, seen):
+        four = []
+        for j in range(4):
+            tile = flat[pl.ds(q * 4 + j, MEMBERS, stride=32), :]
+            seen = jnp.where(lanes % 32 == q * 4 + j, jnp.take_along_axis(tile, wanted, axis=1), seen)
+            four.append(jnp.take_along_axis(tile, swapped, axis=1))
+        four = exchange_four(four, 0, lanes)
+        for j in range(4):
+            tiles_f[q * 4 + j] = four[j]
+        return seen
+
+    seen = lax.fori_loop(0, 8, first_pass, jnp.zeros((MEMBERS, 128), f32))
+
+    table[...] = jnp.zeros_like(table)
+    table[0:4, 0:BATCH] = place_ref[...].astype(f32)
+    table[8:12, 0:BATCH] = order_ref[...].astype(f32)
+    table[16:20, 0:BATCH] = value_ref[...]
+    table[24:28, 0:BATCH] = noise_ref[...]
+    orders = table[8:16, :].T
     wide = lax.broadcasted_iota(jnp.int32, (BATCH, 128), 1)
     wide_f = wide.astype(f32)
     row_block = (region // 16).astype(f32)
     lane_column = (lax.rem(region, 4) * 2 + (wide % 8) // 4).astype(f32)
-    lane_y = (wide // 8) % 4
-    part[...] = jnp.zeros_like(part)
+    lane_batch = wide // 32
+    wide_row = wide[:1]
+    down_here = jnp.float32(0.0)
+    foot = jnp.zeros((1, 128), f32)
+    for i in range(4):
+        down_here = jnp.where(lax.rem(region // 4, 4) == i, down_ref[i], down_here)
+        foot = jnp.where(wide_row % 4 == i, across_ref[i], foot)
+    foot = foot * down_here
+    heights = []
+    for c in range(8):
+        row = jnp.zeros((1, 128), f32)
+        for l in range(4):
+            row = jnp.where((wide_row // 8) % 4 == l, height_ref[l, c], row)
+        heights.append(row)
+    weights = []
     for k in range(4):
-        place = group_ref[k]
-        order = turned_table[:BATCH, 4 + k:5 + k] == wide_f
+        order = orders[:BATCH, k:k + 1] == wide_f
 
         def ordered(row, order=order):
-            return jnp.sum(jnp.where(order, table[row:row + 1], 0.0), axis=1, keepdims=True)
+            return jnp.sum(jnp.where(order, table[row:row + 1, :], 0.0), axis=1, keepdims=True)
 
         picked = ordered(k)
-        value = ordered(8 + k)
-        noise = ordered(12 + k) * 79.0
+        value = ordered(16 + k)
+        noise = ordered(24 + k) * 79.0
         channel = jnp.floor(picked * (1.0 / 64.0))
         site = picked - channel * 64.0
         down = jnp.floor(site * 0.125)
         along = site - down * 8.0
-        cut = jnp.sum(jnp.where(channel == wide_f, table[16:17], 0.0), axis=1, keepdims=True)
+        cut = jnp.zeros((BATCH, 1), f32)
         height = jnp.zeros((BATCH, 128), f32)
         for c in range(8):
-            height = jnp.where(channel == float(c), table[24 + c:25 + c], height)
-        hit = (down == row_block) & (along == lane_column) & (lane_y == place // RING)
-        weights = jnp.where(hit, height * table[17:18], 0.0)
+            here = channel == float(c)
+            cut = jnp.where(here, limit_ref[c].astype(f32), cut)
+            height = jnp.where(here, heights[c], height)
+        hit = (down == row_block) & (along == lane_column) & (lane_batch == k)
+        weights.append(jnp.where(hit, height * foot, 0.0))
         rows = pl.ds(k * BATCH, BATCH)
-        part[rows, :MEMBERS] = lax.dot_general(
-            weights, tiles_f[lax.rem(place, RING)], (((1,), (1,)), ((), ())),
-            precision=highest, preferred_element_type=f32)
         terms[0, rows, :] = jnp.broadcast_to(value, (BATCH, 128))
         terms[1, rows, :] = jnp.broadcast_to(noise, (BATCH, 128))
         terms[2, rows, :] = jnp.broadcast_to(jnp.sqrt(noise), (BATCH, 128))
         terms[3, rows, :] = jnp.broadcast_to(1.0 / (cut + 1.0), (BATCH, 128))
+
+    part[...] = jnp.zeros_like(part)
+    part[:, :MEMBERS] = lax.dot_general(
+        jnp.concatenate(weights), seen, (((1,), (1,)), ((), ())),
+        precision=highest, preferred_element_type=f32)
+
+    @pl.loop(0, 8, unroll=2)
+    def _(q):
+        four = exchange_four([tiles_f[q + 8 * j] for j in range(4)], 5, lanes)
+        for j in range(4):
+            tiles_f[q + 8 * j] = four[j]
+
+    @pl.loop(0, 16, unroll=4)
+    def _(q):
+        low = (q // 4) * 8 + lax.rem(q, 4)
+        a, b = exchange(tiles_f[low], tiles_f[low + 4], 2, lanes)
+        tiles_b[low] = a.astype(bf16)
+        tiles_b[low + 4] = b.astype(bf16)
 
     pl.semaphore_wait(barrier, 61)
 
@@ -273,14 +310,19 @@
         far.append(away_from(region))
 
         def chunk(c, carry, batch=batch, fixed=far[1:]):
-            tiles, means, near = carry
+            tiles, means, near, ahead = carry
             start = pl.multiple_of(batch * BATCH + c * CHUNK, CHUNK)
             block = [terms[i, pl.ds(start, CHUNK), :] for i in range(4)]
             for u in range(CHUNK):
                 value, noise, root_noise, inverse_cut = [b[u:u + 1] for b in block]
-                own = jnp.broadcast_to(tiles[0][:, u:u + 1], (MEMBERS, 128))
-                own_mean = jnp.broadcast_to(means[0][:, u:u + 1], (1, 128))
+                own, own_mean = ahead[0]
+                raw = [(across_lanes(tiles[0], u + AHEAD), across_lanes(means[0], u + AHEAD))]
                 gain, innovation = step_terms(own, own_mean, value, noise, root_noise)
+                ahead_new = []
+                for x, m in ahead[1:] + raw:
+                    cov = column_sum(x * own)
+                    ahead_new.append((x - own * (cov * gain), m + cov * innovation))
+                ahead = ahead_new
                 new_tiles, new_means = [], []
                 for x, m, distance in zip(tiles, means, [near] + fixed):
                     cov = column_sum(x * own) * jnp.maximum(0.0, 1.0 - distance * inverse_cut)
@@ -289,9 +331,10 @@
                 tiles, means = new_tiles, new_means
             tiles = [roll(tiles[0], -CHUNK)] + tiles[1:]
             means = [roll(means[0], -CHUNK)] + means[1:]
-            return tiles, means, roll(near, -CHUNK)
-
-        tiles, means, _ = lax.fori_loop(0, BATCH // CHUNK, chunk, (tiles, means, far[0]))
+            return tiles, means, roll(near, -CHUNK), ahead
+
+        ahead = [(across_lanes(tiles[0], j), across_lanes(means[0], j)) for j in range(AHEAD)]
+        tiles, means, _, _ = lax.fori_loop(0, BATCH // CHUNK, chunk, (tiles, means, far[0], ahead))
         if batch % 2 == 1:
             tiles, means = tiles[1:], means[1:]
         forward(2 * batch)
@@ -357,25 +400,16 @@
     measured_amounts,
     measurement_noise_spread,
 ):
-    row = lax.axis_index("region") // 4
-    down = jnp.sum(jnp.where(jnp.arange(4) == row % 4, sensor_spread_down, 0.0))
-
-    def widen(a):
-        return jnp.pad(a.astype(f32), ((0, 0), (0, 128 - a.shape[1])))
-
-    table = jnp.concatenate([
-        widen(measurement_placement), widen(measurement_ordering),
-        widen(measured_amounts), widen(measurement_noise_spread),
-        widen(taper_radius_limit[None]), jnp.tile(sensor_spread_across * down, 32)[None],
-        jnp.zeros((6, 128), f32), jnp.repeat(channel_height_kernel, 32, axis=1)])
     vmem = pl.BlockSpec(memory_space=pltpu.VMEM)
+    smem = pl.BlockSpec(memory_space=pltpu.SMEM)
     dma = pltpu.SemaphoreType.DMA
     result = pl.pallas_call(
         kernel,
         out_shape=jax.ShapeDtypeStruct((4, MEMBERS, 1024), bf16),
-        in_specs=[vmem, vmem, pl.BlockSpec(memory_space=pltpu.SMEM)],
+        in_specs=[vmem] * 5 + [smem] * 5,
         out_specs=vmem,
         scratch_shapes=[
+            pltpu.VMEM((32, 128), f32),
             pltpu.VMEM((MEMBERS * 32, 128), f32),
             pltpu.VMEM((32, MEMBERS, 128), f32),
             pltpu.VMEM((32, MEMBERS, 128), bf16),
@@ -392,8 +426,11 @@
             dma((32,)), dma((32,)), dma((8, 4)), dma((8, 4)),
         ],
         compiler_params=pltpu.CompilerParams(
-            collective_id=0, has_side_effects=True, vmem_limit_bytes=32 * 1024 * 1024),
-    )(background_members, table, group_area_number)
+            collective_id=0, has_side_effects=True, vmem_limit_bytes=62 * 1024 * 1024),
+    )(
+        background_members, measurement_placement, measurement_ordering, measured_amounts,
+        measurement_noise_spread, channel_height_kernel.T, sensor_spread_down, sensor_spread_across,
+        taper_radius_limit, group_area_number)
     return jnp.transpose(result, (1, 0, 2))[:, :, None, :]
 
 

time: 104 us -> 73.3 us (0.70)
  Pallas kernels: 94.6 us -> 70.7 us
  local copies, waits for them, and re-layouts: 7.53 us -> 2.43 us
  other arithmetic: 1.27 us -> 0 us
    pallas_call x1, Pallas kernels: 94.6 us -> 70.7 us  [body(): pl.pallas_call(kernel, out_shape=jax.ShapeDtypeStruct((4, MEMBERS, 1024),...]
    unnamed x21 -> x0, local copies, waits for them, and re-layouts: 5.82 us -> none
    broadcast_in_dim x1, local copies, waits for them, and re-layouts: 1.34 us -> 2.43 us  [body(): return jnp.transpose(result, (1, 0, 2))[:, :, None, :]]
where the time goes in v3:
time: 73.3 us; the launch traced here: 73.2 us
  Pallas kernels  70.7 us (96%)
  local copies, waits for them, and re-layouts  2.43 us (3%)
    pallas_call x1, Pallas kernels, body(): pl.pallas_call(kernel, out_shape=jax.ShapeDtypeStruct((4, MEMBERS, 1024),...  70.7 us
    broadcast_in_dim x1, local copies, waits for them, and re-layouts, body(): return jnp.transpose(result, (1, 0, 2))[:, :, None, :]  2.43 us

profile of v3, /device:TPU:1, one launch (start us, length us, event | category | flops | bytes accessed | tf_op | source)
XLA Modules:
  0.0 73.2 jit_solution(1881432597305369102)
XLA Ops:
  0.0 70.7 %shard_map.100 = bf16[4,80,1024]{2,1,0:T(8,128)(2,1)} custom-call(bf16[80,4,8,128]{3,2,1,0:T(8,128)(2,1)} %x_ref.1, s32[4,64]{1,0:T(4,128)} %place_ref.1, s32[4,64]{1,0:T(4,128)} %order_ref.1, f32[4,64]{1,0:T(4,128)} %value_ref.1, f32[4,64]{1,0:T(4,128)} %noise_ref.1, f32[4,8]{1,0:T(4,128)} %bitcast.5, f32[4]{0:T(128)} %down_ref.1, f32[4]{0:T(128)} %across_ref.1, ...), custom_call_target="tpu_custom_call" | custom-call | tf_op jit(solution)/shard_map/pallas_call | solution.py:406
  70.7 2.4 %copy.11 = bf16[80,4,1,1024]{3,1,2,0:T(4,128)(2,1)} copy(bf16[80,4,1,1024]{3,0,1,2:T(8,128)(2,1)} %bitcast.4) | data formatting | bytes 1310720 | tf_op jit(solution)/shard_map/broadcast_in_dim | solution.py:434

commit v4 on v3

--- a/solution.py
+++ b/solution.py
@@ -58,7 +58,7 @@
     height_ref, down_ref, across_ref, limit_ref, group_ref, out_ref,
     table, flat, tiles_f, tiles_b, recv_z, turned, recv_y,
     part, total, recv1, recv2, priors, terms,
-    s1, r1, s2, r2, s3, r3, sz, rz, sy, ry,
+    halves, s1, r1, s2, r2, s3, r3, s4, r4, sz, rz, sy, ry,
 ):
     region = lax.axis_index("region")
     lev = lax.axis_index("lev")
@@ -66,11 +66,11 @@
     zc = lax.rem(region, RING)
     z = zc // 2
     core = lax.rem(zc, 2)
-    slab = lev * 8 + yy * 2 + core
+    slab = lev * 4 + yy
 
     def slab_peer(o):
-        g = lax.rem(slab + o, 32)
-        return (lax.rem(g // 2, 4) * RING + z * 2 + lax.rem(g, 2), g // 8)
+        g = lax.rem(slab + o, 16)
+        return (lax.rem(g, 4) * RING + zc, g // 4)
 
     def far_z(h):
         e = h // 2
@@ -89,7 +89,10 @@
 
     barrier = pltpu.get_barrier_semaphore()
 
-    @pl.loop(1, 32)
+    partner = (yy * RING + z * 2 + 1 - core, lev)
+    pl.semaphore_signal(barrier, inc=1, device_id=partner, device_id_type=MESH)
+
+    @pl.loop(1, 16)
     def _(o):
         pl.semaphore_signal(barrier, inc=1, device_id=slab_peer(o), device_id_type=MESH)
 
@@ -188,12 +191,12 @@
         tiles_b[low] = a.astype(bf16)
         tiles_b[low + 4] = b.astype(bf16)
 
-    pl.semaphore_wait(barrier, 61)
+    pl.semaphore_wait(barrier, 46)
 
     def copy1(o):
-        row = pl.multiple_of(lax.rem(slab + o, 32) * 8, 8)
+        row = pl.multiple_of(lax.rem(slab + o, 16) * 8, 8)
         return pltpu.make_async_remote_copy(
-            src_ref=part.at[pl.ds(row, 8)], dst_ref=recv1.at[o],
+            src_ref=halves.at[1, pl.ds(row, 8)], dst_ref=recv1.at[o],
             send_sem=s1.at[o], recv_sem=r1.at[o], device_id=slab_peer(o), device_id_type=MESH)
 
     def copy2(o):
@@ -202,10 +205,19 @@
             send_sem=s2.at[o], recv_sem=r2.at[o], device_id=line_peer(o), device_id_type=MESH)
 
     mine = pl.multiple_of(slab * 8, 8)
+    kept = pl.multiple_of(core * 128, 128)
+    given = pl.multiple_of(128 - core * 128, 128)
+    placed = pl.multiple_of(core * 128 + slab * 8, 8)
+    to_partner = pltpu.make_async_remote_copy(
+        src_ref=part.at[pl.ds(given, 128)], dst_ref=halves.at[0],
+        send_sem=s4.at[0], recv_sem=r4.at[0], device_id=partner, device_id_type=MESH)
+    back_to_partner = pltpu.make_async_remote_copy(
+        src_ref=priors.at[pl.ds(kept, 128)], dst_ref=priors.at[pl.ds(kept, 128)],
+        send_sem=s4.at[1], recv_sem=r4.at[1], device_id=partner, device_id_type=MESH)
 
     def copy3(o):
         return pltpu.make_async_remote_copy(
-            src_ref=total.at[1], dst_ref=priors.at[pl.ds(mine, 8)],
+            src_ref=total.at[1], dst_ref=priors.at[pl.ds(placed, 8)],
             send_sem=s3.at[o], recv_sem=r3.at[o], device_id=slab_peer(o), device_id_type=MESH)
 
     def copy_z(other):
@@ -224,7 +236,11 @@
             src_ref=turned.at[block, to], dst_ref=recv_y.at[yy, block],
             send_sem=sy.at[block, o], recv_sem=ry.at[block, o], device_id=y_peer(o), device_id_type=MESH)
 
-    @pl.loop(1, 32)
+    to_partner.start()
+    to_partner.wait_recv()
+    halves[1] = part[pl.ds(kept, 128), :] + halves[0]
+
+    @pl.loop(1, 16)
     def _(o):
         copy1(o).start()
 
@@ -238,13 +254,13 @@
         copy1(o).wait_recv()
         return acc + recv1[o]
 
-    total[0] = lax.fori_loop(1, 32, add1, part[pl.ds(mine, 8), :])
+    total[0] = lax.fori_loop(1, 16, add1, halves[1, pl.ds(mine, 8), :])
 
     @pl.loop(1, 16)
     def _(o):
         copy2(o).start()
 
-    @pl.loop(12, 30)
+    @pl.loop(12, 20)
     def _(h):
         copy_z(far_z(h)).start()
 
@@ -256,27 +272,31 @@
 
     total[1] = lax.fori_loop(1, 16, add2, total[0])
 
-    @pl.loop(1, 32)
+    @pl.loop(1, 16)
     def _(o):
         copy3(o).start()
 
-    priors[pl.ds(mine, 8), :] = total[1]
-
-    @pl.loop(1, 32)
+    @pl.loop(20, 30)
+    def _(h):
+        copy_z(far_z(h)).start()
+
+    priors[pl.ds(placed, 8), :] = total[1]
+
+    @pl.loop(1, 16)
     def _(o):
         copy3(o).wait_recv()
 
-    def forward(e):
+    back_to_partner.start()
+    back_to_partner.wait_recv()
+
+    def forward(e, first=False):
         away = (e + 1) // 2
-        block = lax.rem(z // 2 + (away if e % 2 else 8 - away), 8)
-        if e == 0:
-            @pl.loop(1, 4)
-            def _(u):
-                arrived_z(block * 4 + lax.rem(zc + u, 4))
-        else:
-            @pl.loop(0, 4)
-            def _(u):
-                arrived_z(block * 4 + u)
+        block = lax.rem(z // 2 + away + lax.rem(e + 1, 2) * (8 - 2 * away), 8)
+
+        @pl.loop(1 if first else 0, 4)
+        def _(u):
+            arrived_z(block * 4 + (lax.rem(zc + u, 4) if first else u))
+
         four = [recv_z[block * 4 + j].astype(f32) for j in range(4)]
         four = exchange_four(four, 3, lanes)
         for j in range(4):
@@ -295,76 +315,83 @@
     tiles = [anomaly[:, :128], anomaly[:, 128:], jnp.where(members == lanes, 1.0, 0.0).astype(f32)]
     means = [mean[:, :128], mean[:, 128:], jnp.zeros((1, 128), f32)]
     lane_row = lanes[:1]
-    for batch in range(4):
-        here = group_ref[batch]
-
-        def away_from(other, here=here):
-            return jnp.full((1, 128), jnp.abs(other - here), jnp.int32).astype(f32)
-
-        if batch % 2 == 0:
-            far = [jnp.where(lane_row < BATCH, 0.0, away_from(group_ref[batch + 1]))]
-        else:
-            far = [jnp.zeros((1, 128), f32)]
-        if batch < 2:
-            far.append(jnp.where(lane_row < BATCH, away_from(group_ref[2]), away_from(group_ref[3])))
-        far.append(away_from(region))
-
-        def chunk(c, carry, batch=batch, fixed=far[1:]):
-            tiles, means, near, ahead = carry
-            start = pl.multiple_of(batch * BATCH + c * CHUNK, CHUNK)
-            block = [terms[i, pl.ds(start, CHUNK), :] for i in range(4)]
-            for u in range(CHUNK):
-                value, noise, root_noise, inverse_cut = [b[u:u + 1] for b in block]
-                own, own_mean = ahead[0]
-                raw = [(across_lanes(tiles[0], u + AHEAD), across_lanes(means[0], u + AHEAD))]
-                gain, innovation = step_terms(own, own_mean, value, noise, root_noise)
-                ahead_new = []
-                for x, m in ahead[1:] + raw:
-                    cov = column_sum(x * own)
-                    ahead_new.append((x - own * (cov * gain), m + cov * innovation))
-                ahead = ahead_new
-                new_tiles, new_means = [], []
-                for x, m, distance in zip(tiles, means, [near] + fixed):
-                    cov = column_sum(x * own) * jnp.maximum(0.0, 1.0 - distance * inverse_cut)
-                    new_tiles.append(x - own * (cov * gain))
-                    new_means.append(m + cov * innovation)
-                tiles, means = new_tiles, new_means
-            tiles = [roll(tiles[0], -CHUNK)] + tiles[1:]
-            means = [roll(means[0], -CHUNK)] + means[1:]
-            return tiles, means, roll(near, -CHUNK), ahead
-
-        ahead = [(across_lanes(tiles[0], j), across_lanes(means[0], j)) for j in range(AHEAD)]
-        tiles, means, _, _ = lax.fori_loop(0, BATCH // CHUNK, chunk, (tiles, means, far[0], ahead))
-        if batch % 2 == 1:
-            tiles, means = tiles[1:], means[1:]
-        forward(2 * batch)
-        forward(2 * batch + 1)
+    forward(0, first=True)
+    for half in range(2):
+
+        def one_batch(part, carry, half=half):
+            tiles, means = carry
+            batch = half * 2 + part
+            here = group_ref[batch]
+
+            def away_from(other):
+                return jnp.full((1, 128), jnp.abs(other - here), jnp.int32).astype(f32)
+
+            near = jnp.where(lane_row < BATCH, 0.0, away_from(group_ref[half * 2 + 1]))
+            fixed = [away_from(region)]
+            if half == 0:
+                fixed = [jnp.where(lane_row < BATCH, away_from(group_ref[2]), away_from(group_ref[3]))] + fixed
+
+            def chunk(c, carry):
+                tiles, means, near, ahead = carry
+                start = pl.multiple_of(batch * BATCH + c * CHUNK, CHUNK)
+                block = [terms[i, pl.ds(start, CHUNK), :] for i in range(4)]
+                for u in range(CHUNK):
+                    value, noise, root_noise, inverse_cut = [b[u:u + 1] for b in block]
+                    own, own_mean = ahead[0]
+                    raw = [(across_lanes(tiles[0], u + AHEAD), across_lanes(means[0], u + AHEAD))]
+                    gain, innovation = step_terms(own, own_mean, value, noise, root_noise)
+                    ahead_new = []
+                    for x, m in ahead[1:] + raw:
+                        cov = column_sum(x * own)
+                        ahead_new.append((x - own * (cov * gain), m + cov * innovation))
+                    ahead = ahead_new
+                    new_tiles, new_means = [], []
+                    for x, m, distance in zip(tiles, means, [near] + fixed):
+                        cov = column_sum(x * own) * jnp.maximum(0.0, 1.0 - distance * inverse_cut)
+                        new_tiles.append(x - own * (cov * gain))
+                        new_means.append(m + cov * innovation)
+                    tiles, means = new_tiles, new_means
+                tiles = [roll(tiles[0], -CHUNK)] + tiles[1:]
+                means = [roll(means[0], -CHUNK)] + means[1:]
+                return tiles, means, roll(near, -CHUNK), ahead
+
+            ahead = [(across_lanes(tiles[0], j), across_lanes(means[0], j)) for j in range(AHEAD)]
+            tiles, means, _, _ = lax.fori_loop(0, BATCH // CHUNK, chunk, (tiles, means, near, ahead))
+
+            @pl.loop(2 * batch + 1, jnp.minimum(2 * batch + 3, 8))
+            def _(e):
+                forward(e)
+
+            return tiles, means
+
+        tiles, means = lax.fori_loop(0, 2, one_batch, (tiles, means))
+        tiles, means = tiles[1:], means[1:]
 
     mixing = jnp.where(lanes < MEMBERS, tiles[0] + means[0], 0.0)
     rest = (1.0 - jnp.sum(mixing, axis=1, keepdims=True)) / MEMBERS
     mixing = (mixing + rest)[:, :MEMBERS]
     high = mixing.astype(bf16)
     low = (mixing - high.astype(f32)).astype(bf16)
-
-    @pl.loop(0, 8)
-    def _(block):
-        @pl.loop(1, 4)
-        def _(o):
-            copy_y(block, o).wait_recv()
+    both = jnp.concatenate([high, low])
 
     @pl.loop(0, 8)
     def _(i):
-        source = i // 2
-        half = lax.rem(i, 2)
-        four = []
-        for j in range(4):
-            block = recv_y[source, half * 4 + j]
-            four.append(
-                jnp.dot(high, block, preferred_element_type=f32)
-                + jnp.dot(low, block, preferred_element_type=f32))
+        half = lax.rem(z // 8 + i // 4, 2)
+        source = lax.rem(i, 4)
+
+        @pl.when(source == 0)
+        def _():
+            @pl.loop(0, 12)
+            def _(n):
+                copy_y(half * 4 + n // 3, 1 + lax.rem(n, 3)).wait_recv()
+
+        blocks = jnp.concatenate([recv_y[source, half * 4 + j] for j in range(4)], axis=1)
+        mixed = jnp.dot(both, blocks, preferred_element_type=f32)
+        mixed = mixed[:MEMBERS] + mixed[MEMBERS:]
+        four = [mixed[:, j * 128:(j + 1) * 128] for j in range(4)]
         four = exchange_four(four, 5, lanes)
         for level in range(4):
-            out_ref[level, :, pl.ds(pl.multiple_of(i * 128, 128), 128)] = four[level].astype(bf16)
+            out_ref[level, :, pl.ds(pl.multiple_of((source * 2 + half) * 128, 128), 128)] = four[level].astype(bf16)
 
     copy_z(z * 2 + 1 - core).wait_send()
 
@@ -372,7 +399,10 @@
     def _(h):
         copy_z(far_z(h)).wait_send()
 
-    @pl.loop(1, 32)
+    to_partner.wait_send()
+    back_to_partner.wait_send()
+
+    @pl.loop(1, 16)
     def _(o):
         copy1(o).wait_send()
         copy3(o).wait_send()
@@ -418,12 +448,13 @@
             pltpu.VMEM((4, 8, MEMBERS, 128), bf16),
             pltpu.VMEM((NOBS, 128), f32),
             pltpu.VMEM((2, 8, 128), f32),
-            pltpu.VMEM((32, 8, 128), f32),
+            pltpu.VMEM((16, 8, 128), f32),
             pltpu.VMEM((16, 8, 128), f32),
             pltpu.VMEM((NOBS, 128), f32),
             pltpu.VMEM((4, NOBS, 128), f32),
-            dma((32,)), dma((32,)), dma((16,)), dma((16,)), dma((32,)), dma((32,)),
-            dma((32,)), dma((32,)), dma((8, 4)), dma((8, 4)),
+            pltpu.VMEM((2, 128, 128), f32),
+            dma((16,)), dma((16,)), dma((16,)), dma((16,)), dma((16,)), dma((16,)),
+            dma((2,)), dma((2,)), dma((32,)), dma((32,)), dma((8, 4)), dma((8, 4)),
         ],
         compiler_params=pltpu.CompilerParams(
             collective_id=0, has_side_effects=True, vmem_limit_bytes=62 * 1024 * 1024),

time: 73.3 us -> 70.4 us (0.960); the launches traced: 73.2 us -> 69.1 us
  Pallas kernels: 70.7 us -> 66.7 us
    pallas_call x1, Pallas kernels: 70.7 us -> 66.7 us  [body(): pl.pallas_call(kernel, out_shape=jax.ShapeDtypeStruct((4, MEMBERS, 1024),...]
where the time goes in v4:
time: 70.4 us; the launch traced here: 69.1 us
  Pallas kernels  66.7 us (95%)
  local copies, waits for them, and re-layouts  2.43 us (3%)
    pallas_call x1, Pallas kernels, body(): pl.pallas_call(kernel, out_shape=jax.ShapeDtypeStruct((4, MEMBERS, 1024),...  66.7 us
    broadcast_in_dim x1, local copies, waits for them, and re-layouts, body(): return jnp.transpose(result, (1, 0, 2))[:, :, None, :]  2.43 us

profile of v4, /device:TPU:1, one launch (start us, length us, event | category | flops | bytes accessed | tf_op | source)
XLA Modules:
  0.0 69.1 jit_solution(8800767605807088792)
XLA Ops:
  0.0 66.7 %shard_map.100 = bf16[4,80,1024]{2,1,0:T(8,128)(2,1)} custom-call(bf16[80,4,8,128]{3,2,1,0:T(8,128)(2,1)} %x_ref.1, s32[4,64]{1,0:T(4,128)} %place_ref.1, s32[4,64]{1,0:T(4,128)} %order_ref.1, f32[4,64]{1,0:T(4,128)} %value_ref.1, f32[4,64]{1,0:T(4,128)} %noise_ref.1, f32[4,8]{1,0:T(4,128)} %bitcast.5, f32[4]{0:T(128)} %down_ref.1, f32[4]{0:T(128)} %across_ref.1, ...), custom_call_target="tpu_custom_call" | custom-call | tf_op jit(solution)/shard_map/pallas_call | solution.py:436
  66.7 2.4 %copy.11 = bf16[80,4,1,1024]{3,1,2,0:T(4,128)(2,1)} copy(bf16[80,4,1,1024]{3,0,1,2:T(8,128)(2,1)} %bitcast.4) | data formatting | bytes 1310720 | tf_op jit(solution)/shard_map/broadcast_in_dim | solution.py:465

commit v5 on v4

--- a/solution.py
+++ b/solution.py
@@ -237,18 +237,18 @@
             send_sem=sy.at[block, o], recv_sem=ry.at[block, o], device_id=y_peer(o), device_id_type=MESH)
 
     to_partner.start()
+    copy_z(z * 2 + 1 - core).start()
+
+    @pl.loop(0, 8)
+    def _(h):
+        copy_z(far_z(h)).start()
+
     to_partner.wait_recv()
     halves[1] = part[pl.ds(kept, 128), :] + halves[0]
 
     @pl.loop(1, 16)
     def _(o):
         copy1(o).start()
-
-    copy_z(z * 2 + 1 - core).start()
-
-    @pl.loop(0, 12)
-    def _(h):
-        copy_z(far_z(h)).start()
 
     def add1(o, acc):
         copy1(o).wait_recv()
@@ -260,7 +260,7 @@
     def _(o):
         copy2(o).start()
 
-    @pl.loop(12, 20)
+    @pl.loop(8, 18)
     def _(h):
         copy_z(far_z(h)).start()
 
@@ -276,7 +276,7 @@
     def _(o):
         copy3(o).start()
 
-    @pl.loop(20, 30)
+    @pl.loop(18, 30)
     def _(h):
         copy_z(far_z(h)).start()
 

time: 70.4 us -> 70.8 us (level); the launches traced: 69.1 us -> 70.7 us
  Pallas kernels: 66.7 us -> 68.2 us
    pallas_call x1, Pallas kernels: 66.7 us -> 68.2 us  [body(): pl.pallas_call(kernel, out_shape=jax.ShapeDtypeStruct((4, MEMBERS, 1024),...]
where the time goes in v5:
time: 70.8 us; the launch traced here: 70.7 us
  Pallas kernels  68.2 us (96%)
  local copies, waits for them, and re-layouts  2.43 us (3%)
    pallas_call x1, Pallas kernels, body(): pl.pallas_call(kernel, out_shape=jax.ShapeDtypeStruct((4, MEMBERS, 1024),...  68.2 us
    broadcast_in_dim x1, local copies, waits for them, and re-layouts, body(): return jnp.transpose(result, (1, 0, 2))[:, :, None, :]  2.43 us

profile of v5, /device:TPU:1, one launch (start us, length us, event | category | flops | bytes accessed | tf_op | source)
XLA Modules:
  0.0 70.7 jit_solution(10132817707163786230)
XLA Ops:
  0.0 68.2 %shard_map.100 = bf16[4,80,1024]{2,1,0:T(8,128)(2,1)} custom-call(bf16[80,4,8,128]{3,2,1,0:T(8,128)(2,1)} %x_ref.1, s32[4,64]{1,0:T(4,128)} %place_ref.1, s32[4,64]{1,0:T(4,128)} %order_ref.1, f32[4,64]{1,0:T(4,128)} %value_ref.1, f32[4,64]{1,0:T(4,128)} %noise_ref.1, f32[4,8]{1,0:T(4,128)} %bitcast.5, f32[4]{0:T(128)} %down_ref.1, f32[4]{0:T(128)} %across_ref.1, ...), custom_call_target="tpu_custom_call" | custom-call | tf_op jit(solution)/shard_map/pallas_call | solution.py:436
  68.2 2.4 %copy.11 = bf16[80,4,1,1024]{3,1,2,0:T(4,128)(2,1)} copy(bf16[80,4,1,1024]{3,0,1,2:T(8,128)(2,1)} %bitcast.4) | data formatting | bytes 1310720 | tf_op jit(solution)/shard_map/broadcast_in_dim | solution.py:465
